TPU v7x, 768 devices: a whole 4x8x12 slice. The times are simulated.
768 devices in a mesh: grp: 16 (over y, core), rank: 48 (over z, x).
Axes of the slice: x: 4, y: 8, z: 12, core: 2. Of those that a mesh axis runs over, the one named last changes fastest.
Arguments:
- a_blocks: bfloat16 [6144, 8, 128, 128], P(('grp', 'rank')), may hold values from -0.5 to 0.5
- a_cols: int32 [6144, 8], P(('grp', 'rank')), may hold values from 0 to 6143, as said below
- p_blocks: bfloat16 [6144, 128, 128], P(('grp', 'rank')), may hold values from -1.796875 to 1.796875
- agg_grp: int32 [6144], P(('grp', 'rank')), may hold values from 0 to 15
- c_slot: int32 [6144, 8], P(('grp', 'rank')), may hold values from 0 to 1
Outputs:
- coarse: bfloat16 [768, 2, 128, 128], P(('grp', 'rank'))
Inputs may be any that keep to these rules, and one draw needn't show every extreme that they name: a_cols[n, 0] = n. Every column lies in the group of its row: a_cols[n, k] // (8 * 48) = n // (8 * 48). For each device and each other device of its group, all columns of the first device's rows that lie on the second device name one and the same row of it.
All inputs are finite; a program needn't handle non-finite values.
Results may differ from a plain program's by a relative error of at most 0.0049.
Values may be sent and summed in bfloat16 or wider, within the bound.
A program may use at most 64 MiB of HBM per device.

v0:
```python
import jax
import jax.numpy as jnp
from jax import lax
from jax.sharding import PartitionSpec as P

SLOTS = 2


def on_device(a_blocks, a_cols, p_blocks, agg_grp, c_slot):
    rows = a_blocks.shape[0]
    width = a_blocks.shape[1]
    order = p_blocks.shape[1]
    entries = rows * width
    ranks = lax.axis_size("rank")
    flat_cols = a_cols.reshape(-1)
    peer = flat_cols // rows % ranks
    within = flat_cols % rows
    wanted = peer * rows + within
    piece = lax.all_gather(p_blocks, "rank", axis=0, tiled=True)
    count = piece.shape[0]
    select = (wanted[:, None] == jnp.arange(count, dtype=jnp.int32)[None, :]).astype(jnp.bfloat16)
    chosen = jnp.einsum("en,nxy->exy", select, piece, preferred_element_type=jnp.float32).astype(
        jnp.bfloat16
    )
    chosen = chosen.reshape(rows, width, order, order)
    product = jnp.einsum(
        "qkxy,qkyz->qkxz", a_blocks, chosen, preferred_element_type=jnp.float32
    ).astype(jnp.bfloat16)
    term = jnp.einsum("qyx,qkyz->qkxz", p_blocks, product, preferred_element_type=jnp.float32)
    flat_term = term.reshape(entries, order, order)
    target = jnp.broadcast_to(agg_grp[:, None], (rows, width)).reshape(-1)
    slots = c_slot.reshape(-1)
    slot_iota = jnp.arange(SLOTS, dtype=jnp.int32)
    row_iota = jnp.arange(lax.axis_size("grp") * 1, dtype=jnp.int32)
    hit = (target[:, None, None] == row_iota[None, :, None]) & (
        slots[:, None, None] == slot_iota[None, None, :]
    )
    table = hit.reshape(entries, lax.axis_size("grp") * 1 * SLOTS).astype(jnp.float32)
    summed = jnp.einsum("et,exy->txy", table, flat_term, precision=lax.Precision.HIGHEST)
    coarse = lax.psum_scatter(
        summed.reshape(lax.axis_size("grp") * 1, SLOTS, order, order),
        "grp",
        scatter_dimension=0,
        tiled=True,
    )
    return coarse.astype(jnp.bfloat16)


def solution(mesh):
    in_specs = (
        P(("grp", "rank"), None, None, None),
        P(("grp", "rank"), None),
        P(("grp", "rank"), None, None),
        P(("grp", "rank")),
        P(("grp", "rank"), None),
    )
    out_specs = P(("grp", "rank"), None, None, None)
    return jax.shard_map(
        on_device, mesh=mesh, in_specs=in_specs, out_specs=out_specs, check_vma=False
    )
```

profile of v0, /device:TPU:1, one launch (start us, length us, event | category | flops | bytes accessed | tf_op | source)
XLA Modules:
  0.0 279.4 jit_solution(17420016223809491389)
XLA Ops:
  6.5 0.0 copy-start
  6.5 0.0 all-gather.2.cloned.1.call-start
  6.5 2.0 copy.13
  8.5 0.0 all-gather.2.cloned.1.call-update
  8.5 0.0 reduce-scatter.2.cloned.1.call-start
  8.6 0.8 reshape.124
  9.4 0.7 broadcast_in_dim.2
  10.1 0.1 eq.56
  10.2 0.8 eq.60
  11.1 0.0 copy-start.1
  11.1 170.8 %all-gather.2.cloned.1.call-done = bf16[384,128,128]{2,0,1:T(8,128)(2,1)} async-done(((bf16[8,128,128]{2,0,1:T(8,128)(2,1)}), bf16[384,128,128]{2,0,1:T(8,128)(2,1)}) %all-gather.2.cloned.1.call-update) | async-done | bytes 12582928 | tf_op jit(solution)/shard_map/all_gather | solution.py:19
  181.9 8.2 %convert_bitcast_fusion = bf16[8,8,128,128]{3,1,0,2:T(8,128)(2,1)} fusion(bf16[384,128,128]{2,0,1:T(8,128)(2,1)} %all-gather.2.cloned.1.call-done, s32[64]{0:T(128)S(1)} %fusion.16), kind=kOutput, calls=%fused_computation.7 | convolution fusion | flops 806379520 | bytes 14680320 | tf_op jit(solution)/shard_map/en,nxy->exy/dot_general | solution.py:22
  190.1 0.0 copy-done
  190.1 0.0 copy-done.1
  190.1 6.2 %fusion.2 = f32[8,8,128,128]{3,2,1,0:T(8,128)} fusion(bf16[8,8,128,128]{3,2,1,0:T(8,128)(2,1)S(1)} %copy-done, bf16[8,8,128,128]{3,1,0,2:T(8,128)(2,1)} %convert_bitcast_fusion, bf16[8,128,128]{2,1,0:T(8,128)(2,1)S(1)} %copy-done.1), kind=kOutput, calls=%fused_computation.2 | convolution fusion | flops 537919488 | bytes 8650752 | tf_op jit(solution)/shard_map/qyx,qkyz->qkxz/dot_general | solution.py:29
  196.3 5.4 %copy.16 = f32[64,128,128]{2,0,1:T(8,128)} copy(f32[64,128,128]{1,2,0:T(8,128)} %bitcast.25) | data formatting | bytes 8388608 | tf_op jit(solution)/shard_map/reshape | solution.py:30
  201.7 3.8 %fusion = f32[16,2,128,128]{3,0,2,1:T(8,128)S(1)} fusion(f32[64,128,128]{2,0,1:T(8,128)} %copy.16, pred[16,2,64,1]{2,1,0,3:T(4,128)(4,1)S(1)} %bitcast.26), kind=kOutput, calls=%fused_computation | convolution fusion | flops 402653184 | bytes 6293504 | tf_op jit(solution)/shard_map/et,exy->txy/dot_general | solution.py:39
  205.5 2.0 copy.17
  207.5 0.0 reduce-scatter.2.cloned.1.call-update
  207.5 63.5 %reduce-scatter.2.cloned.1.call-done = f32[1,2,128,128]{3,2,1,0:T(8,128)} async-done(((f32[16,2,128,128]{3,2,1,0:T(8,128)}), f32[1,2,128,128]{3,2,1,0:T(8,128)}) %reduce-scatter.2.cloned.1.call-update) | async-done | bytes 131088 | tf_op jit(solution)/shard_map/reduce_scatter | solution.py:40
  271.0 1.5 convert_element_type.17
  (6 shorter events, 0.1 us)
Async XLA Ops:
  6.5 183.6 %copy-start = (bf16[8,8,128,128]{3,2,1,0:T(8,128)(2,1)S(1)}, bf16[8,8,128,128]{3,2,1,0:T(8,128)(2,1)}, u32[]{:S(2)}) copy-start(bf16[8,8,128,128]{3,2,1,0:T(8,128)(2,1)} %param.5) | copy-start | bytes 6291460
  6.5 175.3 %all-gather.2.cloned.1.call-start = ((), (), s32[]{:S(2)}) async-start(), calls=%async_computation.1 | async-start | bytes 12845056 | tf_op jit(solution)/shard_map/all_gather | solution.py:19
  8.5 262.4 %reduce-scatter.2.cloned.1.call-start = ((), (), s32[]{:S(2)}) async-start(), calls=%async_computation.2 | async-start | bytes 2228224 | tf_op jit(solution)/shard_map/reduce_scatter | solution.py:40
  11.1 179.0 %copy-start.1 = (bf16[8,128,128]{2,1,0:T(8,128)(2,1)S(1)}, bf16[8,128,128]{2,1,0:T(8,128)(2,1)}, u32[]{:S(2)}) copy-start(bf16[8,128,128]{2,1,0:T(8,128)(2,1)} %param.7) | copy-start | bytes 786436
Sparse Core Ops, SparseCore 0:
  10.9 170.9 all-gather.1
  207.7 63.2 reduce-scatter.1
where the time goes:
time: 280 us; the launch traced here: 279 us
  waiting for transfers between devices  234 us (84%)
  matrix products  18.2 us (6%)
  between operations  13.4 us (5%)
  local copies, waits for them, and re-layouts  11.8 us (4%)
    all_gather x1, waiting for transfers between devices, on_device(): piece = lax.all_gather(p_blocks, 'rank', axis=0, tiled=True)  171 us
    reduce_scatter x1, waiting for transfers between devices, on_device(): lax.psum_scatter(summed.reshape(lax.axis_size('grp') * 1, SLOTS, order, o...  63.5 us
    dot_general x1, matrix products, on_device(): jnp.einsum('en,nxy->exy', select, piece, preferred_element_type=jnp.float32)  8.23 us
    dot_general x1, matrix products, on_device(): jnp.einsum('qyx,qkyz->qkxz', p_blocks, product, preferred_element_type=jn...  6.21 us
  transfers between devices with their start and end apart: 2, of which 2 were waited for; matrix products, arithmetic and copies ran while one was open for 1% of the time, Pallas kernels for 0%

commit v1 on v0

v1 whole, which is shorter than its diff:
```python
import functools

import jax
import jax.numpy as jnp
from jax import lax
from jax.experimental import pallas as pl
from jax.experimental.pallas import tpu as pltpu
from jax.sharding import PartitionSpec as P

SLOTS = 2
CORES = 2
X = 4
Z = 12
CHUNKS = 4
STAGGER = 2

MESH = pl.DeviceIdType.MESH
NT = (((1,), (1,)), ((), ()))


def kernel(
    sizes,
    cols,
    agg,
    slot,
    p_ref,
    a_hbm,
    out_ref,
    a_ref,
    ring,
    stage,
    table,
    sums,
    outgoing,
    incoming,
    total,
    table_smem,
    place,
    a_sem,
    table_sem,
    table_send,
    table_recv,
    ring_send,
    ring_recv,
    x_send,
    x_recv,
    sum_send,
    sum_recv,
    *chosen,
):
    xs, zs, groups, rows, width, order, chunks, stagger = sizes
    ys = groups // CORES
    half = zs // 2
    part = order // chunks
    ranks = xs * zs
    grp = lax.axis_index("grp")
    rank = lax.axis_index("rank")
    z, x = lax.div(rank, xs), lax.rem(rank, xs)
    y, core = lax.div(grp, CORES), lax.rem(grp, CORES)

    def rank_at(dx, dz):
        return {"rank": lax.rem(z + dz + zs, zs) * xs + lax.rem(x + dx, xs)}

    def grp_at(hop):
        dy, dc = hop // CORES, hop % CORES
        return lax.rem(y + dy, ys) * CORES + lax.rem(core + dc, CORES)

    neighbours = [rank_at(0, 1), rank_at(0, -1)]
    neighbours += [rank_at(d, 0) for d in range(1, xs)]
    neighbours += [{"grp": grp_at(hop)} for hop in range(1, groups)]
    barrier = pltpu.get_barrier_semaphore()
    for device in neighbours:
        pl.semaphore_signal(barrier, inc=1, device_id=device, device_id_type=MESH)
    a_copy = pltpu.make_async_copy(a_hbm, a_ref, a_sem)
    a_copy.start()

    for w in range(rows):
        turned = p_ref[w].astype(jnp.float32).T.astype(jnp.bfloat16)
        for c in range(chunks):
            ring[c, 0, w] = turned[c * part : (c + 1) * part]

    lane = lax.broadcasted_iota(jnp.int32, (8, 128), 1)
    base = grp * (ranks * rows)

    def want(e, held):
        local = cols[lax.div(e, width), lax.rem(e, width)] - base
        peer, within = lax.div(local, rows), lax.rem(local, rows)
        rx = lax.rem(lax.rem(peer, xs) - x + xs, xs)
        j = lax.rem(z - lax.div(peer, xs) + zs, zs)
        spot = jnp.where(j < half, 2 * j - 1, 2 * (zs - j))
        spot = jnp.where(j == 0, 0, jnp.where(j == half, zs - 1, spot))
        place[e] = jnp.where(peer == rank, ranks + within, rx * zs + spot)
        return jnp.maximum(held, jnp.where(lane == peer, within, 0))

    table[0] = lax.fori_loop(0, rows * width, want, jnp.zeros((8, 128), jnp.int32))

    pl.semaphore_wait(barrier, len(neighbours))

    def table_copy(d):
        return pltpu.make_async_remote_copy(
            src_ref=table.at[0],
            dst_ref=table.at[xs - d],
            send_sem=table_send.at[d - 1],
            recv_sem=table_recv.at[xs - d - 1],
            device_id=rank_at(d, 0),
            device_id_type=MESH,
        )

    def ring_copy(c, s, down):
        if down:
            src, dst = (zs - s + 1) % zs, zs - s
        else:
            src, dst = s - 1, s
        source, target = ring.at[c, src], ring.at[c, dst]
        if s == half:
            which = pl.ds(down * (rows // 2), rows // 2)
            source, target = source.at[which], target.at[which]
        return pltpu.make_async_remote_copy(
            src_ref=source,
            dst_ref=target,
            send_sem=ring_send.at[c, s - 1, down],
            recv_sem=ring_recv.at[c, s - 1, down],
            device_id=rank_at(0, -1 if down else 1),
            device_id_type=MESH,
        )

    def x_copy(c, d, start, count):
        return pltpu.make_async_remote_copy(
            src_ref=stage.at[c, d - 1, pl.ds(start, count)],
            dst_ref=chosen[c].at[pl.ds((xs - d) * zs + start, count)],
            send_sem=x_send.at[c, d - 1],
            recv_sem=x_recv.at[c, xs - d - 1],
            device_id=rank_at(d, 0),
            device_id_type=MESH,
        )

    def sum_copy(c, hop):
        return pltpu.make_async_remote_copy(
            src_ref=outgoing.at[c, hop - 1],
            dst_ref=incoming.at[c, hop - 1],
            send_sem=sum_send.at[c],
            recv_sem=sum_recv.at[c],
            device_id={"grp": grp_at(hop)},
            device_id_type=MESH,
        )

    def pick(blocks, index):
        held = blocks[0]
        for w in range(1, rows):
            held = jnp.where(index == w, blocks[w], held)
        return held

    def step(c, s):
        if s > 0:
            ring_copy(c, s, 0).wait_recv()
            ring_copy(c, s, 1).wait_recv()
        if s < half:
            ring_copy(c, s + 1, 0).start()
            ring_copy(c, s + 1, 1).start()
        if c == 0 and s == 0:
            for d in range(1, xs):
                table_copy(d).wait_recv()
            fetch = pltpu.make_async_copy(table, table_smem, table_sem)
            fetch.start()
            fetch.wait()
        if s == 0 or s == half:
            hops = [s]
        else:
            hops = [s, zs - s]
        start = 0 if s == 0 else 2 * s - 1
        for at, j in enumerate(hops):
            blocks = [ring[c, j, w] for w in range(rows)]
            spot = start + at
            source = lax.rem(z - j + zs, zs) * xs + x
            if j == 0:
                for w in range(rows):
                    chosen[c][ranks + w] = blocks[w]
                chosen[c][0] = blocks[0]
            else:
                chosen[c][spot] = pick(blocks, table_smem[0, 0, source])
            for d in range(1, xs):
                stage[c, d - 1, spot] = pick(blocks, table_smem[d, 0, source])
        for d in range(1, xs):
            x_copy(c, d, start, len(hops)).start()

    def compute(c):
        for d in range(1, xs):
            x_copy(c, d, 0, zs).wait_recv()

        def row(n, carry):
            products = []
            for k in range(width):
                q = chosen[c][place[n * width + k]]
                product = lax.dot_general(
                    q, a_ref[n * width + k], NT, preferred_element_type=jnp.float32
                )
                products.append(product.astype(jnp.bfloat16))
            term = jnp.dot(
                jnp.concatenate(products, axis=0),
                p_ref[n],
                preferred_element_type=jnp.float32,
            )
            for s in range(SLOTS):
                held = jnp.zeros((part, order), jnp.float32)
                for k in range(width):
                    mine = term[k * part : (k + 1) * part]
                    held = held + jnp.where(slot[n, k] == s, mine, 0.0)
                sums[n, s] = held
            return carry

        lax.fori_loop(0, rows, row, 0)
        mine = pl.ds(c * part, part)
        for hop in range(groups):
            target = grp_at(hop)
            for s in range(SLOTS):
                held = jnp.zeros((part, order), jnp.float32)
                for n in range(rows):
                    held = held + jnp.where(agg[n] == target, sums[n, s], 0.0)
                if hop == 0:
                    total[s, mine] = held
                else:
                    outgoing[c, hop - 1, s] = held.astype(jnp.bfloat16)
            if hop > 0:
                sum_copy(c, hop).start()

    def whole_sum(c):
        return pltpu.make_async_remote_copy(
            src_ref=outgoing.at[c],
            dst_ref=incoming.at[c],
            send_sem=sum_send.at[c],
            recv_sem=sum_recv.at[c],
            device_id={"grp": grp_at(1)},
            device_id_type=MESH,
        )

    def finish(c):
        whole_sum(c).wait_recv()
        mine = pl.ds(c * part, part)
        for s in range(SLOTS):
            held = total[s, mine]
            for hop in range(1, groups):
                held = held + incoming[c, hop - 1, s].astype(jnp.float32)
            total[s, mine] = held

    for d in range(1, xs):
        table_copy(d).start()

    work = []
    for c in range(chunks):
        for s in range(half + 1):
            work.append((s + stagger * c, c, functools.partial(step, c, s)))
        work.append((half + stagger * c + 0.5, c, functools.partial(compute, c)))
    for _, c, task in sorted(work, key=lambda w: w[:2]):
        if task.func is compute and c == 0:
            a_copy.wait()
        task()
    for c in range(chunks):
        finish(c)
    for s in range(SLOTS):
        out_ref[0, s] = total[s].T.astype(jnp.bfloat16)

    for d in range(1, xs):
        table_copy(d).wait_send()
    for c in range(chunks):
        for s in range(1, half + 1):
            ring_copy(c, s, 0).wait_send()
            ring_copy(c, s, 1).wait_send()
        for d in range(1, xs):
            x_copy(c, d, 0, zs).wait_send()
        whole_sum(c).wait_send()


def on_device(xs, zs, a_blocks, a_cols, p_blocks, agg_grp, c_slot):
    rows, width, order = a_blocks.shape[:3]
    groups = lax.axis_size("grp")
    ranks = lax.axis_size("rank")
    part = order // CHUNKS
    half = zs // 2
    sizes = (xs, zs, groups, rows, width, order, CHUNKS, STAGGER)
    smem = pl.BlockSpec(memory_space=pltpu.SMEM)
    vmem = pl.BlockSpec(memory_space=pltpu.VMEM)
    dma = pltpu.SemaphoreType.DMA
    return pl.pallas_call(
        functools.partial(kernel, sizes),
        out_shape=jax.ShapeDtypeStruct((1, SLOTS, order, order), jnp.bfloat16),
        in_specs=[smem, smem, smem, vmem, pl.BlockSpec(memory_space=pl.ANY)],
        out_specs=vmem,
        scratch_shapes=[
            pltpu.VMEM((rows * width, order, order), jnp.bfloat16),
            pltpu.VMEM((CHUNKS, zs, rows, part, order), jnp.bfloat16),
            pltpu.VMEM((CHUNKS, xs - 1, zs, part, order), jnp.bfloat16),
            pltpu.VMEM((xs, 8, 128), jnp.int32),
            pltpu.VMEM((rows, SLOTS, part, order), jnp.float32),
            pltpu.VMEM((CHUNKS, groups - 1, SLOTS, part, order), jnp.bfloat16),
            pltpu.VMEM((CHUNKS, groups - 1, SLOTS, part, order), jnp.bfloat16),
            pltpu.VMEM((SLOTS, order, order), jnp.float32),
            pltpu.SMEM((xs, 8, 128), jnp.int32),
            pltpu.SMEM((rows * width,), jnp.int32),
            dma(()),
            dma(()),
            dma((xs - 1,)),
            dma((xs - 1,)),
            dma((CHUNKS, half, 2)),
            dma((CHUNKS, half, 2)),
            dma((CHUNKS, xs - 1)),
            dma((CHUNKS, xs - 1)),
            dma((CHUNKS,)),
            dma((CHUNKS,)),
        ]
        + [pltpu.VMEM((ranks + rows, part, order), jnp.bfloat16)] * CHUNKS,
        compiler_params=pltpu.CompilerParams(
            collective_id=0, has_side_effects=True, vmem_limit_bytes=40 << 20
        ),
        cost_estimate=pl.CostEstimate(
            flops=4 * rows * width * order**3,
            bytes_accessed=2 * rows * (width + 1) * order**2,
            transcendentals=0,
        ),
    )(a_cols, agg_grp, c_slot, p_blocks, a_blocks.reshape(rows * width, order, order))


def solution(mesh):
    in_specs = (
        P(("grp", "rank"), None, None, None),
        P(("grp", "rank"), None),
        P(("grp", "rank"), None, None),
        P(("grp", "rank")),
        P(("grp", "rank"), None),
    )
    out_specs = P(("grp", "rank"), None, None, None)
    return jax.shard_map(
        functools.partial(on_device, X, Z),
        mesh=mesh,
        in_specs=in_specs,
        out_specs=out_specs,
        check_vma=False,
    )
```

time: 280 us -> 95.4 us (0.34)
  waiting for transfers between devices: 234 us -> 0 us
  Pallas kernels: 0 us -> 89.9 us
  matrix products: 18.2 us -> 0 us
  between operations: 13.4 us -> 0.01 us
  local copies, waits for them, and re-layouts: 11.8 us -> 5.2 us
    all_gather x1 -> x0, waiting for transfers between devices: 171 us -> none  [on_device(): piece = lax.all_gather(p_blocks, 'rank', axis=0, tiled=True)]
    pallas_call x0 -> x1, Pallas kernels: none -> 89.9 us  [on_device(): pl.pallas_call(functools.partial(kernel, sizes), out_shape=jax.ShapeDtype...]
    reduce_scatter x1 -> x0, waiting for transfers between devices: 63.5 us -> none  [on_device(): lax.psum_scatter(summed.reshape(lax.axis_size('grp') * 1, SLOTS, order, o...]
    dot_general x3 -> x0, matrix products: 18.2 us -> none  [the longest x1 8.23 us: on_device(): jnp.einsum('en,nxy->exy', select, piece, preferred_element_type=jnp.float32)]
    reshape x2 -> x0, local copies, waits for them, and re-layouts: 6.17 us -> none  [the longest x1 5.4 us: on_device(): flat_term = term.reshape(entries, order, order)]
    unnamed x5 -> x11, local copies, waits for them, and re-layouts: 1.99 us -> 5.2 us
  transfers between devices with their start and end apart: 2 -> 0, of which waited for: 2 -> 0; matrix products, arithmetic and copies ran while one was open for 1% -> 0% of each run, Pallas kernels for 0% -> 0%
where the time goes in v1:
time: 95.4 us; the launch traced here: 95.2 us
  Pallas kernels  89.9 us (94%)
  local copies, waits for them, and re-layouts  5.2 us (5%)
    pallas_call x1, Pallas kernels, on_device(): pl.pallas_call(functools.partial(kernel, sizes), out_shape=jax.ShapeDtype...  89.9 us
    unnamed x11, local copies, waits for them, and re-layouts  5.2 us

profile of v1, /device:TPU:1, one launch (start us, length us, event | category | flops | bytes accessed | tf_op | source)
XLA Modules:
  0.0 95.2 jit_solution(10319937619547144724)
XLA Ops:
  0.0 0.0 copy-start
  0.0 1.6 %copy-done = bf16[8,8,128,128]{3,2,1,0:T(8,128)(2,1)S(1)} copy-done((bf16[8,8,128,128]{3,2,1,0:T(8,128)(2,1)S(1)}, bf16[8,8,128,128]{3,2,1,0:T(8,128)(2,1)}, u32[]{:S(2)}) %copy-start) | copy-done | bytes 2097176
  1.6 0.0 copy-start.1
  1.6 0.9 copy-done.1
  2.5 0.0 copy-start.2
  2.5 0.7 copy-done.2
  3.2 0.0 copy-start.3
  3.2 0.7 copy-done.3
  3.9 0.0 copy-start.4
  3.9 0.7 copy-done.4
  4.6 89.9 %shard_map.55 = bf16[1,2,128,128]{3,2,1,0:T(8,128)(2,1)S(1)} custom-call(s32[8,8]{1,0:T(8,128)S(1)} %copy-done.2, s32[8]{0:T(128)S(1)} %copy-done.4, s32[8,8]{1,0:T(8,128)S(1)} %copy-done.3, bf16[8,128,128]{2,1,0:T(8,128)(2,1)S(1)} %copy-done.1, bf16[64,128,128]{2,1,0:T(8,128)(2,1)S(1)} %bitcast.1), custom_call_target="tpu_custom_call" | custom-call | flops 536870912 | bytes 2359296 | tf_op jit(solution)/shard_map/pallas_call | solution.py:283
  94.5 0.6 copy.7
Async XLA Ops:
  0.0 1.6 %copy-start = (bf16[8,8,128,128]{3,2,1,0:T(8,128)(2,1)S(1)}, bf16[8,8,128,128]{3,2,1,0:T(8,128)(2,1)}, u32[]{:S(2)}) copy-start(bf16[8,8,128,128]{3,2,1,0:T(8,128)(2,1)} %param.5) | copy-start | bytes 6291460
  1.6 0.9 copy-start.1
  2.5 0.7 copy-start.2
  3.2 0.7 copy-start.3
  3.9 0.7 copy-start.4

commit v2 on v1

v2 whole, which is shorter than its diff:
```python
import functools

import jax
import jax.numpy as jnp
from jax import lax
from jax.experimental import pallas as pl
from jax.experimental.pallas import tpu as pltpu
from jax.sharding import PartitionSpec as P

SLOTS = 2
CORES = 2
X = 4
Z = 12
PARTS = (32, 32, 32, 32)
OFFSETS = (0, 0.5, 1, 1.5)
AHEAD = 10
PIECES = 2
READY = 0.9
GAPS = (0.3, 0.1, 0.7)

MESH = pl.DeviceIdType.MESH
NT = (((1,), (1,)), ((), ()))


def kernel(
    sizes,
    cols_hbm,
    agg_hbm,
    slot_hbm,
    p_hbm,
    a_hbm,
    out_ref,
    cols,
    agg,
    slot,
    p_ref,
    a_ref,
    table,
    sums,
    total,
    table_smem,
    place,
    in_sem,
    table_sem,
    table_send,
    table_recv,
    ring_send,
    ring_recv,
    x_send,
    x_recv,
    sum_send,
    sum_recv,
    pair_send,
    pair_recv,
    *parted,
):
    xs, zs, groups, rows, width, order = sizes
    chunks = len(PARTS)
    firsts = [sum(PARTS[:c]) for c in range(chunks)]
    ring, stage, chosen, outgoing, incoming, pair_out, pair_in, kept = (
        parted[i * chunks : (i + 1) * chunks] for i in range(8)
    )
    ys = groups // CORES
    half = zs // 2
    ranks = xs * zs
    grp = lax.axis_index("grp")
    rank = lax.axis_index("rank")
    z, x = lax.div(rank, xs), lax.rem(rank, xs)
    y, core = lax.div(grp, CORES), lax.rem(grp, CORES)

    def rank_at(dx, dz):
        return {"rank": lax.rem(z + dz + zs, zs) * xs + lax.rem(x + dx, xs)}

    def grp_at(dy, dc=0):
        return lax.rem(y + dy, ys) * CORES + lax.rem(core + dc, CORES)

    neighbours = [rank_at(0, 1), rank_at(0, -1)]
    neighbours += [rank_at(d, 0) for d in range(1, xs)]
    neighbours += [{"grp": grp_at(dy)} for dy in range(1, ys)]
    neighbours += [{"grp": grp_at(0, 1)}]
    barrier = pltpu.get_barrier_semaphore()
    for device in neighbours:
        pl.semaphore_signal(barrier, inc=1, device_id=device, device_id_type=MESH)
    p_copy, cols_copy, agg_copy, slot_copy, a_copy = (
        pltpu.make_async_copy(source, target, in_sem.at[i])
        for i, (source, target) in enumerate(
            [(p_hbm, p_ref), (cols_hbm, cols), (agg_hbm, agg), (slot_hbm, slot), (a_hbm, a_ref)]
        )
    )
    for copy in (p_copy, cols_copy, agg_copy, slot_copy, a_copy):
        copy.start()

    p_copy.wait()
    for w in range(rows):
        turned = p_ref[w].astype(jnp.float32).T.astype(jnp.bfloat16)
        for c in range(chunks):
            ring[c][0, w] = turned[firsts[c] : firsts[c] + PARTS[c]]

    def table_copy(d):
        return pltpu.make_async_remote_copy(
            src_ref=table.at[0],
            dst_ref=table.at[xs - d],
            send_sem=table_send.at[d - 1],
            recv_sem=table_recv.at[xs - d - 1],
            device_id=rank_at(d, 0),
            device_id_type=MESH,
        )

    def ring_copy(c, s, down):
        if down:
            src, dst = (zs - s + 1) % zs, zs - s
        else:
            src, dst = s - 1, s
        source, target = ring[c].at[src], ring[c].at[dst]
        if s == half:
            which = pl.ds(down * (rows // 2), rows // 2)
            source, target = source.at[which], target.at[which]
        return pltpu.make_async_remote_copy(
            src_ref=source,
            dst_ref=target,
            send_sem=ring_send.at[c, s - 1, down],
            recv_sem=ring_recv.at[c, s - 1, down],
            device_id=rank_at(0, -1 if down else 1),
            device_id_type=MESH,
        )

    def x_copy(c, d, start, count):
        return pltpu.make_async_remote_copy(
            src_ref=stage[c].at[d - 1, pl.ds(start, count)],
            dst_ref=chosen[c].at[pl.ds((xs - d) * zs + start, count)],
            send_sem=x_send.at[c, d - 1],
            recv_sem=x_recv.at[c, xs - d - 1],
            device_id=rank_at(d, 0),
            device_id_type=MESH,
        )

    def pair_copy(c):
        return pltpu.make_async_remote_copy(
            src_ref=pair_out[c],
            dst_ref=pair_in[c],
            send_sem=pair_send.at[c],
            recv_sem=pair_recv.at[c],
            device_id={"grp": grp_at(0, 1)},
            device_id_type=MESH,
        )

    def sum_copy(c, dy):
        return pltpu.make_async_remote_copy(
            src_ref=outgoing[c].at[dy - 1],
            dst_ref=incoming[c].at[dy - 1],
            send_sem=sum_send.at[c],
            recv_sem=sum_recv.at[c],
            device_id={"grp": grp_at(dy)},
            device_id_type=MESH,
        )

    def whole_sum(c):
        return pltpu.make_async_remote_copy(
            src_ref=outgoing[c],
            dst_ref=incoming[c],
            send_sem=sum_send.at[c],
            recv_sem=sum_recv.at[c],
            device_id={"grp": grp_at(1)},
            device_id_type=MESH,
        )

    def make_tables():
        cols_copy.wait()
        lane = lax.broadcasted_iota(jnp.int32, (8, 128), 1)
        base = grp * (ranks * rows)

        def row(n, held):
            for k in range(width):
                local = cols[n, k] - base
                peer, within = lax.div(local, rows), lax.rem(local, rows)
                rx = lax.rem(lax.rem(peer, xs) - x + xs, xs)
                j = lax.rem(z - lax.div(peer, xs) + zs, zs)
                spot = jnp.where(j < half, 2 * j - 1, 2 * (zs - j))
                spot = jnp.where(j == 0, 0, jnp.where(j == half, zs - 1, spot))
                place[n * width + k] = jnp.where(
                    peer == rank, ranks + within, rx * zs + spot
                )
                held = jnp.maximum(held, jnp.where(lane == peer, within, 0))
            return held

        table[0] = lax.fori_loop(0, rows, row, jnp.zeros((8, 128), jnp.int32))
        for d in range(1, xs):
            table_copy(d).start()

    def read_tables():
        for d in range(1, xs):
            table_copy(d).wait_recv()
        fetch = pltpu.make_async_copy(table, table_smem, table_sem)
        fetch.start()
        fetch.wait()

    def pick(blocks, index):
        held = blocks[0]
        for w in range(1, rows):
            held = jnp.where(index == w, blocks[w], held)
        return held

    def own(c):
        ring_copy(c, 1, 0).start()
        ring_copy(c, 1, 1).start()

    def step(c, s):
        if s > 0:
            ring_copy(c, s, 0).wait_recv()
            ring_copy(c, s, 1).wait_recv()
            if s < half:
                ring_copy(c, s + 1, 0).start()
                ring_copy(c, s + 1, 1).start()
        if s == 0 or s == half:
            hops = [s]
        else:
            hops = [s, zs - s]
        start = 0 if s == 0 else 2 * s - 1
        for at, j in enumerate(hops):
            blocks = [ring[c][j, w] for w in range(rows)]
            spot = start + at
            source = lax.rem(z - j + zs, zs) * xs + x
            if j == 0:
                for w in range(rows):
                    chosen[c][ranks + w] = blocks[w]
                chosen[c][0] = blocks[0]
            else:
                chosen[c][spot] = pick(blocks, table_smem[0, 0, source])
            for d in range(1, xs):
                stage[c][d - 1, spot] = pick(blocks, table_smem[d, 0, source])
        for d in range(1, xs):
            x_copy(c, d, start, len(hops)).start()

    def multiply(c, piece):
        part = PARTS[c]
        if piece == 0:
            for d in range(1, xs):
                x_copy(c, d, 0, zs).wait_recv()

        def row(n, carry):
            products = []
            for k in range(width):
                q = chosen[c][place[n * width + k]]
                product = lax.dot_general(
                    q, a_ref[n * width + k], NT, preferred_element_type=jnp.float32
                )
                products.append(product.astype(jnp.bfloat16))
            term = jnp.dot(
                jnp.concatenate(products, axis=0),
                p_ref[n],
                preferred_element_type=jnp.float32,
            )
            for s in range(SLOTS):
                held = jnp.zeros((part, order), jnp.float32)
                for k in range(width):
                    mine = term[k * part : (k + 1) * part]
                    held = held + jnp.where(slot[n, k] == s, mine, 0.0)
                sums[n, s, :part] = held
            return carry

        each = rows // PIECES
        lax.fori_loop(piece * each, (piece + 1) * each, row, 0, unroll=True)

    def gather_sums(c, dy, dc, s):
        part = PARTS[c]
        held = jnp.zeros((part, order), jnp.float32)
        for n in range(rows):
            mine = agg[n] == grp_at(dy, dc)
            held = held + jnp.where(mine, sums[n, s, :part], 0.0)
        return held

    def pair_sums(c):
        for dy in range(ys):
            for s in range(SLOTS):
                pair_out[c][dy, s] = gather_sums(c, dy, 1, s).astype(jnp.bfloat16)
        pair_copy(c).start()
        for dy in range(ys):
            for s in range(SLOTS):
                kept[c][dy, s] = gather_sums(c, dy, 0, s)

    def send_sums(c):
        pair_copy(c).wait_recv()
        for dy in sorted(range(1, ys), key=lambda dy: -min(dy, ys - dy)):
            for s in range(SLOTS):
                both = kept[c][dy, s] + pair_in[c][dy, s].astype(jnp.float32)
                outgoing[c][dy - 1, s] = both.astype(jnp.bfloat16)
            sum_copy(c, dy).start()

    def finish(c):
        mine = pl.ds(firsts[c], PARTS[c])
        for s in range(SLOTS):
            total[s, mine] = kept[c][0, s] + pair_in[c][0, s].astype(jnp.float32)
        whole_sum(c).wait_recv()
        for s in range(SLOTS):
            held = total[s, mine]
            for dy in range(1, ys):
                held = held + incoming[c][dy - 1, s].astype(jnp.float32)
            total[s, mine] = held

    pl.semaphore_wait(barrier, len(neighbours))
    work = []

    def put(key, c, call, *args):
        work.append((key, len(work), call, (c, *args)))

    for c in range(chunks):
        put(OFFSETS[c] - AHEAD, c, own)
        for s in range(half + 1):
            put(OFFSETS[c] + s, c, step, s)
        key = OFFSETS[c] + half + READY
        for piece in range(PIECES):
            put(key + GAPS[0] * piece, c, multiply, piece)
        put(key + GAPS[0] + GAPS[1], c, pair_sums)
        put(key + sum(GAPS), c, send_sums)
    work.sort(key=lambda task: task[:2])
    tabled = read = False
    for key, _, call, args in work:
        if call is step and not read:
            make_tables()
            read_tables()
            read = True
        if call is multiply and not tabled:
            for copy in (agg_copy, slot_copy, a_copy):
                copy.wait()
            tabled = True
        call(*args)
    for c in range(chunks):
        finish(c)
    for s in range(SLOTS):
        out_ref[0, s] = total[s].T.astype(jnp.bfloat16)

    for d in range(1, xs):
        table_copy(d).wait_send()
    for c in range(chunks):
        for s in range(1, half + 1):
            ring_copy(c, s, 0).wait_send()
            ring_copy(c, s, 1).wait_send()
        for d in range(1, xs):
            x_copy(c, d, 0, zs).wait_send()
        pair_copy(c).wait_send()
        whole_sum(c).wait_send()


def on_device(xs, zs, a_blocks, a_cols, p_blocks, agg_grp, c_slot):
    rows, width, order = a_blocks.shape[:3]
    groups = lax.axis_size("grp")
    ys = groups // CORES
    ranks = lax.axis_size("rank")
    chunks = len(PARTS)
    half = zs // 2
    sizes = (xs, zs, groups, rows, width, order)
    dma = pltpu.SemaphoreType.DMA

    def parted(*shape, dtype=jnp.bfloat16):
        return [pltpu.VMEM((*shape, part, order), dtype) for part in PARTS]

    return pl.pallas_call(
        functools.partial(kernel, sizes),
        out_shape=jax.ShapeDtypeStruct((1, SLOTS, order, order), jnp.bfloat16),
        in_specs=[pl.BlockSpec(memory_space=pltpu.HBM)] * 5,
        out_specs=pl.BlockSpec(memory_space=pltpu.VMEM),
        scratch_shapes=[
            pltpu.SMEM((rows, width), jnp.int32),
            pltpu.SMEM((rows,), jnp.int32),
            pltpu.SMEM((rows, width), jnp.int32),
            pltpu.VMEM((rows, order, order), jnp.bfloat16),
            pltpu.VMEM((rows * width, order, order), jnp.bfloat16),
            pltpu.VMEM((xs, 8, 128), jnp.int32),
            pltpu.VMEM((rows, SLOTS, max(PARTS), order), jnp.float32),
            pltpu.VMEM((SLOTS, order, order), jnp.float32),
            pltpu.SMEM((xs, 8, 128), jnp.int32),
            pltpu.SMEM((rows * width,), jnp.int32),
            dma((5,)),
            dma(()),
            dma((xs - 1,)),
            dma((xs - 1,)),
            dma((chunks, half, 2)),
            dma((chunks, half, 2)),
            dma((chunks, xs - 1)),
            dma((chunks, xs - 1)),
            dma((chunks,)),
            dma((chunks,)),
            dma((chunks,)),
            dma((chunks,)),
        ]
        + parted(zs, rows)
        + parted(xs - 1, zs)
        + parted(ranks + rows)
        + parted(ys - 1, SLOTS)
        + parted(ys - 1, SLOTS)
        + parted(ys, SLOTS)
        + parted(ys, SLOTS)
        + parted(ys, SLOTS, dtype=jnp.float32),
        compiler_params=pltpu.CompilerParams(
            collective_id=0, has_side_effects=True, vmem_limit_bytes=62 << 20
        ),
        cost_estimate=pl.CostEstimate(
            flops=4 * rows * width * order**3,
            bytes_accessed=2 * rows * (width + 1) * order**2,
            transcendentals=0,
        ),
    )(a_cols, agg_grp, c_slot, p_blocks, a_blocks.reshape(rows * width, order, order))


def solution(mesh):
    in_specs = (
        P(("grp", "rank"), None, None, None),
        P(("grp", "rank"), None),
        P(("grp", "rank"), None, None),
        P(("grp", "rank")),
        P(("grp", "rank"), None),
    )
    out_specs = P(("grp", "rank"), None, None, None)
    return jax.shard_map(
        functools.partial(on_device, X, Z),
        mesh=mesh,
        in_specs=in_specs,
        out_specs=out_specs,
        check_vma=False,
    )
```

time: 95.4 us -> 73 us (0.77)
  Pallas kernels: 89.9 us -> 71 us
  local copies, waits for them, and re-layouts: 5.2 us -> 1.47 us
    pallas_call x1, Pallas kernels: 89.9 us -> 71 us  [on_device(): pl.pallas_call(functools.partial(kernel, sizes), out_shape=jax.ShapeDtype...]
    unnamed x11 -> x1, local copies, waits for them, and re-layouts: 5.2 us -> 1.47 us
where the time goes in v2:
time: 73 us; the launch traced here: 72.5 us
  Pallas kernels  71 us (97%)
  local copies, waits for them, and re-layouts  1.47 us (2%)
    pallas_call x1, Pallas kernels, on_device(): pl.pallas_call(functools.partial(kernel, sizes), out_shape=jax.ShapeDtype...  71 us
    unnamed x1, local copies, waits for them, and re-layouts  1.47 us

profile of v2, /device:TPU:1, one launch (start us, length us, event | category | flops | bytes accessed | tf_op | source)
XLA Modules:
  0.0 72.5 jit_solution(13065018400149264086)
XLA Ops:
  0.0 71.0 %shard_map.55 = bf16[1,2,128,128]{3,2,1,0:T(8,128)(2,1)} custom-call(s32[8,8]{1,0:T(8,128)} %cols_hbm.1, s32[8]{0:T(128)} %agg_hbm.1, s32[8,8]{1,0:T(8,128)} %slot_hbm.1, bf16[8,128,128]{2,1,0:T(8,128)(2,1)} %p_hbm.1, bf16[64,128,128]{2,1,0:T(8,128)(2,1)} %bitcast.1), custom_call_target="tpu_custom_call" | custom-call | flops 536870912 | bytes 2359296 | tf_op jit(solution)/shard_map/pallas_call | solution.py:357
  71.0 1.5 %copy.7 = bf16[1,2,128,128]{3,2,1,0:T(8,128)(2,1)} copy(bf16[1,2,128,128]{3,2,1,0:T(8,128)(2,1)} %shard_map.55) | data formatting | bytes 131072

commit v3 on v2

--- a/solution.py
+++ b/solution.py
@@ -12,11 +12,11 @@
 X = 4
 Z = 12
 PARTS = (32, 32, 32, 32)
-OFFSETS = (0, 0.5, 1, 1.5)
+OFFSETS = (0, 0.6, 1.2, 1.8)
 AHEAD = 10
 PIECES = 2
-READY = 0.9
-GAPS = (0.3, 0.1, 0.7)
+READY = 0.01
+GAPS = (0.2, 0.2, 0.4)
 
 MESH = pl.DeviceIdType.MESH
 NT = (((1,), (1,)), ((), ()))
@@ -52,16 +52,24 @@
     sum_recv,
     pair_send,
     pair_recv,
+    far_send,
+    far_recv,
+    pass_send,
+    pass_recv,
+    late_send,
+    late_recv,
     *parted,
 ):
     xs, zs, groups, rows, width, order = sizes
     chunks = len(PARTS)
     firsts = [sum(PARTS[:c]) for c in range(chunks)]
-    ring, stage, chosen, outgoing, incoming, pair_out, pair_in, kept = (
-        parted[i * chunks : (i + 1) * chunks] for i in range(8)
+    ring, stage, late, passed, chosen, outgoing, incoming, pair_out, pair_in, kept = (
+        parted[i * chunks : (i + 1) * chunks] for i in range(10)
     )
     ys = groups // CORES
     half = zs // 2
+    full, few = half - 2, xs // 2
+    early = 2 * full + 1
     ranks = xs * zs
     grp = lax.axis_index("grp")
     rank = lax.axis_index("rank")
@@ -74,7 +82,7 @@
     def grp_at(dy, dc=0):
         return lax.rem(y + dy, ys) * CORES + lax.rem(core + dc, CORES)
 
-    neighbours = [rank_at(0, 1), rank_at(0, -1)]
+    neighbours = [rank_at(d, dz) for dz in (1, -1) for d in range(xs)]
     neighbours += [rank_at(d, 0) for d in range(1, xs)]
     neighbours += [{"grp": grp_at(dy)} for dy in range(1, ys)]
     neighbours += [{"grp": grp_at(0, 1)}]
@@ -108,16 +116,12 @@
 
     def ring_copy(c, s, down):
         if down:
-            src, dst = (zs - s + 1) % zs, zs - s
+            src, dst = (early - s + 1) % early, early - s
         else:
             src, dst = s - 1, s
-        source, target = ring[c].at[src], ring[c].at[dst]
-        if s == half:
-            which = pl.ds(down * (rows // 2), rows // 2)
-            source, target = source.at[which], target.at[which]
-        return pltpu.make_async_remote_copy(
-            src_ref=source,
-            dst_ref=target,
+        return pltpu.make_async_remote_copy(
+            src_ref=ring[c].at[src],
+            dst_ref=ring[c].at[dst],
             send_sem=ring_send.at[c, s - 1, down],
             recv_sem=ring_recv.at[c, s - 1, down],
             device_id=rank_at(0, -1 if down else 1),
@@ -127,10 +131,67 @@
     def x_copy(c, d, start, count):
         return pltpu.make_async_remote_copy(
             src_ref=stage[c].at[d - 1, pl.ds(start, count)],
-            dst_ref=chosen[c].at[pl.ds((xs - d) * zs + start, count)],
+            dst_ref=chosen[c].at[pl.ds((xs - d) * early + start, count)],
             send_sem=x_send.at[c, d - 1],
             recv_sem=x_recv.at[c, xs - d - 1],
             device_id=rank_at(d, 0),
+            device_id_type=MESH,
+        )
+
+    def far_copy(i):
+        source, target, count = [
+            (0, xs, xs),
+            (0, 2 * xs, xs),
+            (xs + few, 3 * xs + few, xs - few),
+            (2 * xs, 3 * xs, few),
+        ][i]
+        return pltpu.make_async_remote_copy(
+            src_ref=table.at[pl.ds(source, count)],
+            dst_ref=table.at[pl.ds(target, count)],
+            send_sem=far_send.at[i],
+            recv_sem=far_recv.at[i],
+            device_id=rank_at(0, -1 if i % 2 else 1),
+            device_id_type=MESH,
+        )
+
+    def late_copy(c, down, d):
+        return pltpu.make_async_remote_copy(
+            src_ref=late[c].at[down * xs + d],
+            dst_ref=chosen[c].at[xs * early + (xs - d) % xs * 3 + down],
+            send_sem=late_send.at[c, 0],
+            recv_sem=late_recv.at[c],
+            device_id=rank_at(d, -1 if down else 1),
+            device_id_type=MESH,
+        )
+
+    def pass_copy(c, down):
+        count = xs - few if down else few
+        return pltpu.make_async_remote_copy(
+            src_ref=late[c].at[pl.ds(2 * xs + down * few, count)],
+            dst_ref=passed[c].at[pl.ds(down * few, count)],
+            send_sem=pass_send.at[c, down],
+            recv_sem=pass_recv.at[c, down],
+            device_id=rank_at(0, -1 if down else 1),
+            device_id_type=MESH,
+        )
+
+    def last_copy(c, d):
+        return pltpu.make_async_remote_copy(
+            src_ref=passed[c].at[d],
+            dst_ref=chosen[c].at[xs * early + (xs - d) % xs * 3 + 2],
+            send_sem=late_send.at[c, 1],
+            recv_sem=late_recv.at[c],
+            device_id=rank_at(d, 1 if d < few else -1),
+            device_id_type=MESH,
+        )
+
+    def whole_late(c, source, i):
+        return pltpu.make_async_remote_copy(
+            src_ref=source,
+            dst_ref=chosen[c].at[pl.ds(xs * early, source.shape[0])],
+            send_sem=late_send.at[c, i],
+            recv_sem=late_recv.at[c],
+            device_id=rank_at(0, 1),
             device_id_type=MESH,
         )
 
@@ -166,7 +227,7 @@
 
     def make_tables():
         cols_copy.wait()
-        lane = lax.broadcasted_iota(jnp.int32, (8, 128), 1)
+        lane = lax.broadcasted_iota(jnp.int32, (1, 128), 1)
         base = grp * (ranks * rows)
 
         def row(n, held):
@@ -176,23 +237,43 @@
                 rx = lax.rem(lax.rem(peer, xs) - x + xs, xs)
                 j = lax.rem(z - lax.div(peer, xs) + zs, zs)
                 spot = jnp.where(j < half, 2 * j - 1, 2 * (zs - j))
-                spot = jnp.where(j == 0, 0, jnp.where(j == half, zs - 1, spot))
-                place[n * width + k] = jnp.where(
-                    peer == rank, ranks + within, rx * zs + spot
+                spot = jnp.where(j == half, zs - 1, jnp.maximum(spot, 0))
+                spot = jnp.where(
+                    spot < early,
+                    rx * early + spot,
+                    xs * early + rx * 3 + spot - early,
                 )
+                place[n * width + k] = jnp.where(peer == rank, ranks + within, spot)
                 held = jnp.maximum(held, jnp.where(lane == peer, within, 0))
             return held
 
-        table[0] = lax.fori_loop(0, rows, row, jnp.zeros((8, 128), jnp.int32))
+        table[0] = lax.fori_loop(0, rows, row, jnp.zeros((1, 128), jnp.int32))
         for d in range(1, xs):
             table_copy(d).start()
 
     def read_tables():
         for d in range(1, xs):
             table_copy(d).wait_recv()
-        fetch = pltpu.make_async_copy(table, table_smem, table_sem)
+        far_copy(0).start()
+        far_copy(1).start()
+        fetch_tables(0, xs)
+
+    def fetch_tables(start, count):
+        which = pl.ds(start, count)
+        fetch = pltpu.make_async_copy(table.at[which], table_smem.at[which], table_sem)
         fetch.start()
         fetch.wait()
+
+    def pass_tables():
+        far_copy(0).wait_recv()
+        far_copy(1).wait_recv()
+        far_copy(2).start()
+        far_copy(3).start()
+
+    def read_far_tables():
+        far_copy(2).wait_recv()
+        far_copy(3).wait_recv()
+        fetch_tables(xs, 3 * xs)
 
     def pick(blocks, index):
         held = blocks[0]
@@ -204,20 +285,39 @@
         ring_copy(c, 1, 0).start()
         ring_copy(c, 1, 1).start()
 
+    def send_late(c, down):
+        j = half + 2 if down else full
+        source = lax.rem(z - j + zs, zs) * xs + x
+        blocks = [ring[c][early - full if down else full, w] for w in range(rows)]
+        passing = range(few, xs) if down else range(few)
+        for d in passing:
+            late[c][2 * xs + d] = pick(blocks, table_smem[3 * xs + d, 0, source])
+        pass_copy(c, down).start()
+        for d in range(xs):
+            index = table_smem[(1 if down else 2) * xs + d, 0, source]
+            late[c][down * xs + d] = pick(blocks, index)
+            late_copy(c, down, d).start()
+
     def step(c, s):
+        if s == full + 1:
+            for down in (0, 1):
+                pass_copy(c, down).wait_recv()
+                for d in range(few, xs) if down else range(few):
+                    last_copy(c, d).start()
+            return
         if s > 0:
             ring_copy(c, s, 0).wait_recv()
             ring_copy(c, s, 1).wait_recv()
-            if s < half:
-                ring_copy(c, s + 1, 0).start()
-                ring_copy(c, s + 1, 1).start()
-        if s == 0 or s == half:
-            hops = [s]
-        else:
-            hops = [s, zs - s]
+        if s == full:
+            send_late(c, 0)
+            send_late(c, 1)
+        elif s > 0:
+            ring_copy(c, s + 1, 0).start()
+            ring_copy(c, s + 1, 1).start()
+        hops = [(0, 0)] if s == 0 else [(s, s), (zs - s, early - s)]
         start = 0 if s == 0 else 2 * s - 1
-        for at, j in enumerate(hops):
-            blocks = [ring[c][j, w] for w in range(rows)]
+        for at, (j, held) in enumerate(hops):
+            blocks = [ring[c][held, w] for w in range(rows)]
             spot = start + at
             source = lax.rem(z - j + zs, zs) * xs + x
             if j == 0:
@@ -235,7 +335,8 @@
         part = PARTS[c]
         if piece == 0:
             for d in range(1, xs):
-                x_copy(c, d, 0, zs).wait_recv()
+                x_copy(c, d, 0, early).wait_recv()
+            whole_late(c, late[c], 0).wait_recv()
 
         def row(n, carry):
             products = []
@@ -305,13 +406,15 @@
 
     for c in range(chunks):
         put(OFFSETS[c] - AHEAD, c, own)
-        for s in range(half + 1):
+        for s in range(half):
             put(OFFSETS[c] + s, c, step, s)
         key = OFFSETS[c] + half + READY
         for piece in range(PIECES):
             put(key + GAPS[0] * piece, c, multiply, piece)
         put(key + GAPS[0] + GAPS[1], c, pair_sums)
         put(key + sum(GAPS), c, send_sums)
+    work.append((full * 0.4, len(work), pass_tables, ()))
+    work.append((full * 0.9, len(work), read_far_tables, ()))
     work.sort(key=lambda task: task[:2])
     tabled = read = False
     for key, _, call, args in work:
@@ -331,12 +434,18 @@
 
     for d in range(1, xs):
         table_copy(d).wait_send()
+    for i in range(4):
+        far_copy(i).wait_send()
     for c in range(chunks):
-        for s in range(1, half + 1):
+        for s in range(1, full + 1):
             ring_copy(c, s, 0).wait_send()
             ring_copy(c, s, 1).wait_send()
         for d in range(1, xs):
-            x_copy(c, d, 0, zs).wait_send()
+            x_copy(c, d, 0, early).wait_send()
+        whole_late(c, late[c].at[pl.ds(0, 2 * xs)], 0).wait_send()
+        whole_late(c, passed[c], 1).wait_send()
+        for down in (0, 1):
+            pass_copy(c, down).wait_send()
         pair_copy(c).wait_send()
         whole_sum(c).wait_send()
 
@@ -347,7 +456,8 @@
     ys = groups // CORES
     ranks = lax.axis_size("rank")
     chunks = len(PARTS)
-    half = zs // 2
+    full = zs // 2 - 2
+    early = 2 * full + 1
     sizes = (xs, zs, groups, rows, width, order)
     dma = pltpu.SemaphoreType.DMA
 
@@ -356,7 +466,7 @@
 
     return pl.pallas_call(
         functools.partial(kernel, sizes),
-        out_shape=jax.ShapeDtypeStruct((1, SLOTS, order, order), jnp.bfloat16),
+        out_shape=pltpu.VMEM((1, SLOTS, order, order), jnp.bfloat16),
         in_specs=[pl.BlockSpec(memory_space=pltpu.HBM)] * 5,
         out_specs=pl.BlockSpec(memory_space=pltpu.VMEM),
         scratch_shapes=[
@@ -365,26 +475,34 @@
             pltpu.SMEM((rows, width), jnp.int32),
             pltpu.VMEM((rows, order, order), jnp.bfloat16),
             pltpu.VMEM((rows * width, order, order), jnp.bfloat16),
-            pltpu.VMEM((xs, 8, 128), jnp.int32),
+            pltpu.VMEM((4 * xs, 1, 128), jnp.int32),
             pltpu.VMEM((rows, SLOTS, max(PARTS), order), jnp.float32),
             pltpu.VMEM((SLOTS, order, order), jnp.float32),
-            pltpu.SMEM((xs, 8, 128), jnp.int32),
+            pltpu.SMEM((4 * xs, 1, 128), jnp.int32),
             pltpu.SMEM((rows * width,), jnp.int32),
             dma((5,)),
             dma(()),
             dma((xs - 1,)),
             dma((xs - 1,)),
-            dma((chunks, half, 2)),
-            dma((chunks, half, 2)),
+            dma((chunks, full, 2)),
+            dma((chunks, full, 2)),
             dma((chunks, xs - 1)),
             dma((chunks, xs - 1)),
             dma((chunks,)),
             dma((chunks,)),
             dma((chunks,)),
             dma((chunks,)),
+            dma((4,)),
+            dma((4,)),
+            dma((chunks, 2)),
+            dma((chunks, 2)),
+            dma((chunks, 2)),
+            dma((chunks,)),
         ]
-        + parted(zs, rows)
-        + parted(xs - 1, zs)
+        + parted(early, rows)
+        + parted(xs - 1, early)
+        + parted(3 * xs)
+        + parted(xs)
         + parted(ranks + rows)
         + parted(ys - 1, SLOTS)
         + parted(ys - 1, SLOTS)

time: 73 us -> 67.9 us (0.930)
  Pallas kernels: 71 us -> 67.1 us
  local copies, waits for them, and re-layouts: 1.47 us -> 0.63 us
    pallas_call x1, Pallas kernels: 71 us -> 67.1 us  [on_device(): pl.pallas_call(functools.partial(kernel, sizes), out_shape=pltpu.VMEM((1,...]
    unnamed x1, local copies, waits for them, and re-layouts: 1.47 us -> 0.63 us
where the time goes in v3:
time: 67.9 us; the launch traced here: 67.8 us
  Pallas kernels  67.1 us (99%)
    pallas_call x1, Pallas kernels, on_device(): pl.pallas_call(functools.partial(kernel, sizes), out_shape=pltpu.VMEM((1,...  67.1 us

profile of v3, /device:TPU:1, one launch (start us, length us, event | category | flops | bytes accessed | tf_op | source)
XLA Modules:
  0.0 67.8 jit_solution(1151698917099339217)
XLA Ops:
  0.0 67.1 %shard_map.55 = bf16[1,2,128,128]{3,2,1,0:T(8,128)(2,1)S(1)} custom-call(s32[8,8]{1,0:T(8,128)} %cols_hbm.1, s32[8]{0:T(128)} %agg_hbm.1, s32[8,8]{1,0:T(8,128)} %slot_hbm.1, bf16[8,128,128]{2,1,0:T(8,128)(2,1)} %p_hbm.1, bf16[64,128,128]{2,1,0:T(8,128)(2,1)} %bitcast.1), custom_call_target="tpu_custom_call" | custom-call | flops 536870912 | bytes 2359296 | tf_op jit(solution)/shard_map/pallas_call | solution.py:467
  67.1 0.6 copy.7

commit v4 on v3

--- a/solution.py
+++ b/solution.py
@@ -12,14 +12,15 @@
 X = 4
 Z = 12
 PARTS = (32, 32, 32, 32)
-OFFSETS = (0, 0.6, 1.2, 1.8)
+LAG = 0
+LAG_GROWTH = 0.15
 AHEAD = 10
+TURN = 0.08
 PIECES = 2
 READY = 0.01
 GAPS = (0.2, 0.2, 0.4)
 
 MESH = pl.DeviceIdType.MESH
-NT = (((1,), (1,)), ((), ()))
 
 
 def kernel(
@@ -331,6 +332,16 @@
         for d in range(1, xs):
             x_copy(c, d, start, len(hops)).start()
 
+    def turn(n):
+        if n == 0:
+            a_copy.wait()
+
+        def block(e, carry):
+            a_ref[e] = a_ref[e].T
+            return carry
+
+        lax.fori_loop(n * width, (n + 1) * width, block, 0, unroll=4)
+
     def multiply(c, piece):
         part = PARTS[c]
         if piece == 0:
@@ -342,8 +353,8 @@
             products = []
             for k in range(width):
                 q = chosen[c][place[n * width + k]]
-                product = lax.dot_general(
-                    q, a_ref[n * width + k], NT, preferred_element_type=jnp.float32
+                product = jnp.dot(
+                    q, a_ref[n * width + k], preferred_element_type=jnp.float32
                 )
                 products.append(product.astype(jnp.bfloat16))
             term = jnp.dot(
@@ -401,18 +412,21 @@
     pl.semaphore_wait(barrier, len(neighbours))
     work = []
 
-    def put(key, c, call, *args):
+    def put(hop, c, call, *args):
+        key = hop + c * (LAG + LAG_GROWTH * min(max(hop, 0), half))
         work.append((key, len(work), call, (c, *args)))
 
     for c in range(chunks):
-        put(OFFSETS[c] - AHEAD, c, own)
+        put(-AHEAD, c, own)
         for s in range(half):
-            put(OFFSETS[c] + s, c, step, s)
-        key = OFFSETS[c] + half + READY
+            put(s, c, step, s)
+        key = half + READY
         for piece in range(PIECES):
             put(key + GAPS[0] * piece, c, multiply, piece)
         put(key + GAPS[0] + GAPS[1], c, pair_sums)
         put(key + sum(GAPS), c, send_sums)
+    for n in range(rows):
+        work.append((full * (0.2 + TURN * n), len(work), turn, (n,)))
     work.append((full * 0.4, len(work), pass_tables, ()))
     work.append((full * 0.9, len(work), read_far_tables, ()))
     work.sort(key=lambda task: task[:2])
@@ -423,7 +437,7 @@
             read_tables()
             read = True
         if call is multiply and not tabled:
-            for copy in (agg_copy, slot_copy, a_copy):
+            for copy in (agg_copy, slot_copy):
                 copy.wait()
             tabled = True
         call(*args)

time: 67.9 us -> 66.6 us (0.981)
  Pallas kernels: 67.1 us -> 65.8 us
    pallas_call x1, Pallas kernels: 67.1 us -> 65.8 us  [on_device(): pl.pallas_call(functools.partial(kernel, sizes), out_shape=pltpu.VMEM((1,...]
where the time goes in v4:
time: 66.6 us; the launch traced here: 66.4 us
  Pallas kernels  65.8 us (99%)
    pallas_call x1, Pallas kernels, on_device(): pl.pallas_call(functools.partial(kernel, sizes), out_shape=pltpu.VMEM((1,...  65.8 us

profile of v4, /device:TPU:1, one launch (start us, length us, event | category | flops | bytes accessed | tf_op | source)
XLA Modules:
  0.0 66.4 jit_solution(881374095417105343)
XLA Ops:
  0.0 65.8 %shard_map.55 = bf16[1,2,128,128]{3,2,1,0:T(8,128)(2,1)S(1)} custom-call(s32[8,8]{1,0:T(8,128)} %cols_hbm.1, s32[8]{0:T(128)} %agg_hbm.1, s32[8,8]{1,0:T(8,128)} %slot_hbm.1, bf16[8,128,128]{2,1,0:T(8,128)(2,1)} %p_hbm.1, bf16[64,128,128]{2,1,0:T(8,128)(2,1)} %bitcast.1), custom_call_target="tpu_custom_call" | custom-call | flops 536870912 | bytes 2359296 | tf_op jit(solution)/shard_map/pallas_call | solution.py:481
  65.8 0.6 copy.7

commit v5 on v4

--- a/solution.py
+++ b/solution.py
@@ -441,11 +441,8 @@
                 copy.wait()
             tabled = True
         call(*args)
-    for c in range(chunks):
+    for c in range(chunks - 1):
         finish(c)
-    for s in range(SLOTS):
-        out_ref[0, s] = total[s].T.astype(jnp.bfloat16)
-
     for d in range(1, xs):
         table_copy(d).wait_send()
     for i in range(4):
@@ -461,7 +458,12 @@
         for down in (0, 1):
             pass_copy(c, down).wait_send()
         pair_copy(c).wait_send()
-        whole_sum(c).wait_send()
+        if c < chunks - 1:
+            whole_sum(c).wait_send()
+    finish(chunks - 1)
+    for s in range(SLOTS):
+        out_ref[0, s] = total[s].T.astype(jnp.bfloat16)
+    whole_sum(chunks - 1).wait_send()
 
 
 def on_device(xs, zs, a_blocks, a_cols, p_blocks, agg_grp, c_slot):

time: 66.6 us -> 66.5 us (level)
  no operation moved by 1% of the time
where the time goes in v5:
time: 66.5 us; the launch traced here: 66.3 us
  Pallas kernels  65.7 us (99%)
    pallas_call x1, Pallas kernels, on_device(): pl.pallas_call(functools.partial(kernel, sizes), out_shape=pltpu.VMEM((1,...  65.7 us

profile of v5, /device:TPU:1, one launch (start us, length us, event | category | flops | bytes accessed | tf_op | source)
XLA Modules:
  0.0 66.3 jit_solution(2925352432685442777)
XLA Ops:
  0.0 65.7 %shard_map.55 = bf16[1,2,128,128]{3,2,1,0:T(8,128)(2,1)S(1)} custom-call(s32[8,8]{1,0:T(8,128)} %cols_hbm.1, s32[8]{0:T(128)} %agg_hbm.1, s32[8,8]{1,0:T(8,128)} %slot_hbm.1, bf16[8,128,128]{2,1,0:T(8,128)(2,1)} %p_hbm.1, bf16[64,128,128]{2,1,0:T(8,128)(2,1)} %bitcast.1), custom_call_target="tpu_custom_call" | custom-call | flops 536870912 | bytes 2359296 | tf_op jit(solution)/shard_map/pallas_call | solution.py:483
  65.7 0.6 copy.7
